TPU v7x, 512 devices: a whole 4x4x16 slice. The times are simulated.
512 devices in a mesh: tm: 16 (over x, y), tile: 32 (over z, core).
Axes of the slice: x: 4, y: 4, z: 16, core: 2. Of those that a mesh axis runs over, the one named last changes fastest.
Arguments:
- haar_video: bfloat16 [64, 128, 6144], P('tm', 'tile'), may hold values from -6 to 6
- clip_lengths: int32 [16], replicated, may hold values from 1 to 8, 64 in all
- block_owner: int32 [16], replicated, may hold values from 0 to 15, each once
- spatial_in: bfloat16 [3, 3, 48, 128], replicated, may hold values from -0.3125 to 0.3125
- temporal_in: bfloat16 [3, 128, 128], replicated, may hold values from -0.3125 to 0.3125
- bias_in: float32 [128], replicated, may hold values from -4 to 4
- spatial_down: bfloat16 [3, 3, 128, 256], replicated, may hold values from -0.25 to 0.25
- temporal_down: bfloat16 [3, 256, 256], replicated, may hold values from -0.25 to 0.25
- bias_down: float32 [256], replicated, may hold values from -4 to 4
- spatial_out: bfloat16 [3, 3, 256, 256], replicated, may hold values from -0.1875 to 0.1875
- temporal_out: bfloat16 [3, 256, 256], replicated, may hold values from -0.25 to 0.25
- bias_out: float32 [256], replicated, may hold values from -3 to 3
Outputs:
- latents: bfloat16 [32, 64, 64, 256], P('tm', 'tile')
Inputs may be any that keep to these rules, and one draw needn't show every extreme that they name: `clip_lengths`: the clip lengths sum to 64; the longest is exactly 8. `block_owner`: every tm index is named exactly once.
All inputs are finite; a program needn't handle non-finite values.
Results may differ from a plain program's by a relative error of at most 0.015.
Values may be sent and summed in bfloat16 or wider, within the bound.
A program may use at most 64 MiB of HBM per device.

v0:
```python
from functools import partial
import jax
import jax.numpy as jnp
from jax import lax
from jax.sharding import PartitionSpec as P


def padded_2(block, sides, width):
    for axis, dim in sides:
        count = lax.axis_size(axis)
        forward = [(i, i + 1) for i in range(count - 1)]
        backward = [(target, source) for source, target in forward]
        low = lax.ppermute(
            lax.slice_in_dim(block, block.shape[dim] - width, None, axis=dim), axis, forward
        )
        high = lax.ppermute(lax.slice_in_dim(block, 0, width, axis=dim), axis, backward)
        block = jnp.concatenate([low, block, high], axis=dim)
    return block


def passed_along(block, axis, distance):
    devices = range(lax.axis_size(axis))
    route = [(i - distance, i) for i in devices if i - distance in devices]
    return lax.ppermute(block, axis, route)


def clip_of(frame_ids, clip_lengths):
    clip_ends = jnp.cumsum(clip_lengths)
    return jnp.sum((clip_ends[None, :] <= frame_ids[:, None]).astype(jnp.int32), axis=1)


def tap_mask(key_frames, tap_frames, clip_lengths):
    tap_clips = clip_of(tap_frames.reshape(-1), clip_lengths).reshape(tap_frames.shape)
    same_clip = tap_clips == clip_of(key_frames, clip_lengths)[:, None]
    return jnp.where(same_clip & (tap_frames >= 0), 1.0, 0.0).astype(jnp.bfloat16)


def spatial_conv(row_extended, kernel, stride, out_rows, out_cols):
    pad_right = 1 if stride == 1 else 0
    padded = jnp.pad(row_extended, ((0, 0), (0, 0), (1, pad_right), (0, 0)))
    pieces = [
        padded[
            :,
            row_tap : row_tap + stride * out_rows : stride,
            col_tap : col_tap + stride * out_cols : stride,
        ]
        for row_tap in range(3)
        for col_tap in range(3)
    ]
    patches = jnp.concatenate(pieces, axis=-1)
    flattened = jnp.dot(
        patches.reshape(-1, patches.shape[-1]),
        kernel.reshape(-1, kernel.shape[-1]),
        preferred_element_type=jnp.float32,
    )
    return flattened.reshape(patches.shape[:-1] + (kernel.shape[-1],))


def temporal_conv(extended, kernel, mask, out_count, stride, bias, activate):
    running = None
    for lag in range(3):
        tap_frames = extended[lag : lag + stride * out_count : stride] * mask[:, lag].reshape(
            (-1, 1, 1, 1)
        )
        tap_term = jnp.dot(
            tap_frames.reshape(-1, tap_frames.shape[-1]),
            kernel[lag],
            preferred_element_type=jnp.float32,
        )
        running = tap_term if running is None else running + tap_term
    running = running + bias
    if activate:
        running = jax.nn.silu(running)
    return running.reshape(tap_frames.shape[:-1] + (kernel.shape[-1],)).astype(jnp.bfloat16)


def pick_rows(running, shard_piece, first_row, owners, my_index, block_span):
    row_total = shard_piece.shape[0]
    row_ids = jnp.arange(row_total, dtype=jnp.int32)
    block_ids = row_ids // block_span
    slot_ids = jnp.arange(owners.shape[0], dtype=jnp.int32)
    owner_of = jnp.sum(
        jnp.where(block_ids[:, None] == slot_ids[None, :], owners[None, :], 0), axis=1
    )
    position = row_ids % block_span
    span_ids = jnp.arange(block_span, dtype=jnp.int32)
    select = ((position[None, :] == span_ids[:, None]) & (owner_of[None, :] == my_index)).astype(
        jnp.bfloat16
    )
    return jnp.dot(select, shard_piece, preferred_element_type=jnp.float32)


def third_mask(block_index, reduced_count, clip_lengths):
    reduced_ids = block_index * reduced_count + jnp.arange(reduced_count, dtype=jnp.int32)
    lags = jnp.arange(3, dtype=jnp.int32)
    reduced_taps = reduced_ids[:, None] + lags[None, :] - 2
    return tap_mask(2 * reduced_ids + 1, 2 * reduced_taps + 1, clip_lengths)


def per_device(
    haar_video,
    clip_lengths,
    block_owner,
    spatial_in,
    temporal_in,
    bias_in,
    spatial_down,
    temporal_down,
    bias_down,
    spatial_out,
    temporal_out,
    bias_out,
):
    frame_count, row_count, flat_width = haar_video.shape
    in_channels = spatial_in.shape[2]
    col_count = flat_width // in_channels
    frames = haar_video.reshape(frame_count, row_count, col_count, in_channels)
    my_index = lax.axis_index("tm")
    lags = jnp.arange(3, dtype=jnp.int32)
    row_extended = padded_2(frames, (("tile", 1),), 1)
    spatial_one = spatial_conv(row_extended, spatial_in, 1, row_count, col_count).astype(
        jnp.bfloat16
    )
    context = passed_along(spatial_one[frame_count - 2 :], "tm", 1)
    extended = jnp.concatenate([context, spatial_one], axis=0)
    frame_ids = my_index * frame_count + jnp.arange(frame_count, dtype=jnp.int32)
    causal_mask = tap_mask(frame_ids, frame_ids[:, None] + lags[None, :] - 2, clip_lengths)
    hidden_one = temporal_conv(extended, temporal_in, causal_mask, frame_count, 1, bias_in, True)
    upper_row = passed_along(hidden_one[:, row_count - 1 :], "tile", 1)
    row_extended = jnp.concatenate([upper_row, hidden_one], axis=1)
    reduced_rows = row_count // 2
    reduced_cols = col_count // 2
    reduced_count = frame_count // 2
    spatial_two = spatial_conv(row_extended, spatial_down, 2, reduced_rows, reduced_cols).astype(
        jnp.bfloat16
    )
    prior_frame = passed_along(spatial_two[frame_count - 1 :], "tm", 1)
    extended = jnp.concatenate([prior_frame, spatial_two], axis=0)
    reduced_ids = my_index * reduced_count + jnp.arange(reduced_count, dtype=jnp.int32)
    strided_mask = tap_mask(
        2 * reduced_ids + 1, 2 * reduced_ids[:, None] + lags[None, :] - 1, clip_lengths
    )
    hidden_two = temporal_conv(
        extended, temporal_down, strided_mask, reduced_count, 2, bias_down, True
    )
    context = passed_along(hidden_two, "tm", 1)
    extended = jnp.concatenate([context, hidden_two], axis=0)
    block_span = extended.shape[0]
    flattened = extended.reshape(block_span, -1)
    gather_fn = partial(pick_rows, owners=block_owner, my_index=my_index, block_span=block_span)
    moved_block = gather_fn(
        jnp.zeros(flattened.shape, jnp.float32),
        lax.all_gather(flattened, "tm", axis=0, tiled=True),
        jnp.int32(0),
    )
    moved_block = moved_block.astype(jnp.bfloat16).reshape(extended.shape)
    slot_ids = jnp.arange(block_owner.shape[0], dtype=jnp.int32)
    source_block = jnp.sum(jnp.where(block_owner == my_index, slot_ids, 0))
    row_extended = padded_2(moved_block, (("tile", 1),), 1)
    spatial_three = spatial_conv(row_extended, spatial_out, 1, reduced_rows, reduced_cols).astype(
        jnp.bfloat16
    )
    last_mask = third_mask(source_block, reduced_count, clip_lengths)
    final_block = temporal_conv(
        spatial_three, temporal_out, last_mask, reduced_count, 1, bias_out, False
    )
    return final_block


def solution(mesh):
    placed = (P("tm", "tile", None), P(), P(), P(), P(), P(), P(), P(), P(), P(), P(), P())
    return jax.shard_map(
        per_device,
        mesh=mesh,
        in_specs=placed,
        out_specs=P("tm", "tile", None, None),
        check_vma=False,
    )
```

profile of v0, /device:TPU:97, one launch (start us, length us, event | category | flops | bytes accessed | tf_op | source)
XLA Modules:
  0.0 164.6 jit_solution(17710069117527432567)
XLA Ops:
  6.5 1.5 reshape.216
  8.3 5.3 %collective-permute-start = (bf16[4,1,128,48]{2,3,1,0:T(8,128)(2,1)S(1)}, bf16[4,1,128,48]{2,3,1,0:T(8,128)(2,1)S(1)}, u32[]{:S(2)}, u32[]{:S(2)}) collective-permute-start(bf16[4,1,128,48]{2,3,1,0:T(8,128)(2,1)S(1)} %get-tuple-element.28), channel_id=1, source_target_pairs={{0,1},{1,2},{2,3},{3,4},{4,5},{5,6},{6,7},{7,8},{8,9},{9,10},{10,1... | collective-permute-start | bytes 147464 | tf_op jit(solution)/shard_map/ppermute | solution.py:13
  13.6 1.9 %collective-permute-start.1 = (bf16[4,1,128,48]{2,3,1,0:T(8,128)(2,1)S(1)}, bf16[4,1,128,48]{2,3,1,0:T(8,128)(2,1)S(1)}, u32[]{:S(2)}, u32[]{:S(2)}) collective-permute-start(bf16[4,1,128,48]{2,3,1,0:T(8,128)(2,1)S(1)} %get-tuple-element.29), channel_id=1, source_target_pairs={{1,0},{2,1},{3,2},{4,3},{5,4},{6,5},{7,6},{8,7},{9,8},{10,9},{11,1... | collective-permute-start | bytes 147464 | tf_op jit(solution)/shard_map/ppermute | solution.py:16
  17.1 1.3 fusion.55
  19.4 0.8 collective-permute-done.1
  21.4 0.8 convolution_convert_fusion.1
  22.3 3.2 %collective-permute-start.2 = (bf16[2,4,128,128]{3,2,1,0:T(8,128)(2,1)S(1)}, bf16[2,4,128,128]{3,2,1,0:T(8,128)(2,1)S(1)}, u32[]{:S(2)}, u32[]{:S(2)}) collective-permute-start(bf16[2,4,128,128]{3,2,1,0:T(8,128)(2,1)S(1)} %slice.252), channel_id=1, source_target_pairs={{0,32},{32,64},{64,96},{96,128},{128,160},{160,192},{192,224},{224... | collective-permute-start | bytes 786440 | tf_op jit(solution)/shard_map/ppermute | solution.py:24
  26.2 4.0 %collective-permute-done.2 = bf16[2,4,128,128]{3,2,1,0:T(8,128)(2,1)S(1)} collective-permute-done((bf16[2,4,128,128]{3,2,1,0:T(8,128)(2,1)S(1)}, bf16[2,4,128,128]{3,2,1,0:T(8,128)(2,1)S(1)}, u32[]{:S(2)}, u32[]{:S(2)}) %collective-permute-start.2) | collective-permute-done | bytes 262176 | tf_op jit(solution)/shard_map/ppermute | solution.py:24
  31.6 4.4 %collective-permute-start.3 = (bf16[4,1,128,128]{3,2,1,0:T(8,128)(2,1)S(1)}, bf16[4,1,128,128]{3,2,1,0:T(8,128)(2,1)S(1)}, u32[]{:S(2)}, u32[]{:S(2)}) collective-permute-start(bf16[4,1,128,128]{3,2,1,0:T(8,128)(2,1)S(1)} %slice.255), channel_id=1, source_target_pairs={{0,1},{1,2},{2,3},{3,4},{4,5},{5,6},{6,7},{7,8},{8,9},{9,10},{10,1... | collective-permute-start | bytes 393224 | tf_op jit(solution)/shard_map/ppermute | solution.py:24
  36.2 1.6 collective-permute-done.3
  40.9 0.8 slice.214
  43.4 4.1 %collective-permute-start.4 = (bf16[1,2,64,256]{3,2,1,0:T(8,128)(2,1)S(1)}, bf16[1,2,64,256]{3,2,1,0:T(8,128)(2,1)S(1)}, u32[]{:S(2)}, u32[]{:S(2)}) collective-permute-start(bf16[1,2,64,256]{3,2,1,0:T(8,128)(2,1)S(1)} %slice.256), channel_id=1, source_target_pairs={{0,32},{32,64},{64,96},{96,128},{128,160},{160,192},{192,224},{224... | collective-permute-start | bytes 196616 | tf_op jit(solution)/shard_map/ppermute | solution.py:24
  47.6 1.2 collective-permute-done.4
  49.6 3.8 %collective-permute-start.5 = (bf16[2,2,64,256]{3,2,1,0:T(8,128)(2,1)S(1)}, bf16[2,2,64,256]{3,2,1,0:T(8,128)(2,1)S(1)}, u32[]{:S(2)}, u32[]{:S(2)}) collective-permute-start(bf16[2,2,64,256]{3,2,1,0:T(8,128)(2,1)S(1)} %bitcast.94), channel_id=1, source_target_pairs={{0,32},{32,64},{64,96},{96,128},{128,160},{160,192},{192,224},{224... | collective-permute-start | bytes 393224 | tf_op jit(solution)/shard_map/ppermute | solution.py:24
  53.4 2.7 %collective-permute-done.5 = bf16[2,2,64,256]{3,2,1,0:T(8,128)(2,1)S(1)} collective-permute-done((bf16[2,2,64,256]{3,2,1,0:T(8,128)(2,1)S(1)}, bf16[2,2,64,256]{3,2,1,0:T(8,128)(2,1)S(1)}, u32[]{:S(2)}, u32[]{:S(2)}) %collective-permute-start.5) | collective-permute-done | bytes 131104 | tf_op jit(solution)/shard_map/ppermute | solution.py:24
  56.2 0.9 reshape.236
  57.2 75.2 %all-gather.3.cloned.1.call-done = bf16[16,4,32768]{2,1,0:T(4,128)(2,1)} async-done(((bf16[1,4,32768]{2,1,0:T(4,128)(2,1)}), bf16[16,4,32768]{2,1,0:T(4,128)(2,1)}) %all-gather.3.cloned.1.call-update) | async-done | bytes 4194320 | tf_op jit(solution)/shard_map/all_gather | solution.py:153
  132.4 7.0 %reshape.237 = bf16[64,32768]{1,0:T(8,128)(2,1)} reshape(bf16[16,4,32768]{2,1,0:T(4,128)(2,1)} %all-gather.3.cloned.1.call-done) | data formatting | bytes 8388608
  139.4 2.8 %convolution_convert_fusion = bf16[4,32768]{1,0:T(4,128)(2,1)S(1)} fusion(bf16[64,32768]{1,0:T(8,128)(2,1)} %reshape.237, s32[64]{0:T(128)S(1)} %and_select_fusion.3, pred[64]{0:T(512)(128)(4,1)S(1)} %broadcast_compare_fusion), kind=kOutput, calls=%fused_computation | convolution fusion | flops 16908800 | bytes 4456768 | tf_op jit(solution)/shard_map/dot_general | solution.py:90
  142.3 5.0 %collective-permute-start.6 = (bf16[4,1,64,256]{3,2,1,0:T(8,128)(2,1)S(1)}, bf16[4,1,64,256]{3,2,1,0:T(8,128)(2,1)S(1)}, u32[]{:S(2)}, u32[]{:S(2)}) collective-permute-start(bf16[4,1,64,256]{3,2,1,0:T(8,128)(2,1)S(1)} %get-tuple-element.24), channel_id=1, source_target_pairs={{0,1},{1,2},{2,3},{3,4},{4,5},{5,6},{6,7},{7,8},{8,9},{9,10},{10,1... | collective-permute-start | bytes 393224 | tf_op jit(solution)/shard_map/ppermute | solution.py:13
  147.3 1.9 %collective-permute-start.7 = (bf16[4,1,64,256]{3,2,1,0:T(8,128)(2,1)S(1)}, bf16[4,1,64,256]{3,2,1,0:T(8,128)(2,1)S(1)}, u32[]{:S(2)}, u32[]{:S(2)}) collective-permute-start(bf16[4,1,64,256]{3,2,1,0:T(8,128)(2,1)S(1)} %get-tuple-element.25), channel_id=1, source_target_pairs={{1,0},{2,1},{3,2},{4,3},{5,4},{6,5},{7,6},{8,7},{9,8},{10,9},{11,1... | collective-permute-start | bytes 393224 | tf_op jit(solution)/shard_map/ppermute | solution.py:16
  149.5 5.3 %collective-permute-done.7 = bf16[4,1,64,256]{3,2,1,0:T(8,128)(2,1)S(1)} collective-permute-done((bf16[4,1,64,256]{3,2,1,0:T(8,128)(2,1)S(1)}, bf16[4,1,64,256]{3,2,1,0:T(8,128)(2,1)S(1)}, u32[]{:S(2)}, u32[]{:S(2)}) %collective-permute-start.7) | collective-permute-done | bytes 131104 | tf_op jit(solution)/shard_map/ppermute | solution.py:16
  155.4 0.8 convolution_convert_fusion.2
  156.9 0.8 fusion.7
  (113 shorter events, 12.7 us)
Async XLA Ops:
  6.5 148.8 %copy-start = (bf16[3,3,256,256]{3,2,1,0:T(8,128)(2,1)S(1)}, bf16[3,3,256,256]{3,2,1,0:T(8,128)(2,1)}, u32[]{:S(2)}) copy-start(bf16[3,3,256,256]{3,2,1,0:T(8,128)(2,1)} %param.21) | copy-start | bytes 3538948
  6.5 125.9 %all-gather.3.cloned.1.call-start = ((), (), s32[]{:S(2)}) async-start(), calls=%async_computation | async-start | bytes 4456448 | tf_op jit(solution)/shard_map/all_gather | solution.py:153
  8.3 11.1 %collective-permute-start = (bf16[4,1,128,48]{2,3,1,0:T(8,128)(2,1)S(1)}, bf16[4,1,128,48]{2,3,1,0:T(8,128)(2,1)S(1)}, u32[]{:S(2)}, u32[]{:S(2)}) collective-permute-start(bf16[4,1,128,48]{2,3,1,0:T(8,128)(2,1)S(1)} %get-tuple-element.28), channel_id=1, source_target_pairs={{0,1},{1,2},{2,3},{3,4},{4,5},{5,6},{6,7},{7,8},{8,9},{9,10},{10,1... | collective-permute-start | bytes 147464 | tf_op jit(solution)/shard_map/ppermute | solution.py:13
  13.6 6.6 %collective-permute-start.1 = (bf16[4,1,128,48]{2,3,1,0:T(8,128)(2,1)S(1)}, bf16[4,1,128,48]{2,3,1,0:T(8,128)(2,1)S(1)}, u32[]{:S(2)}, u32[]{:S(2)}) collective-permute-start(bf16[4,1,128,48]{2,3,1,0:T(8,128)(2,1)S(1)} %get-tuple-element.29), channel_id=1, source_target_pairs={{1,0},{2,1},{3,2},{4,3},{5,4},{6,5},{7,6},{8,7},{9,8},{10,9},{11,1... | collective-permute-start | bytes 147464 | tf_op jit(solution)/shard_map/ppermute | solution.py:16
  20.5 0.9 copy-start.3
  22.3 8.2 %copy-start.4 = (bf16[3,128,128]{2,1,0:T(8,128)(2,1)S(1)}, bf16[3,128,128]{2,1,0:T(8,128)(2,1)}, u32[]{:S(2)}) copy-start(bf16[3,128,128]{2,1,0:T(8,128)(2,1)} %param.16) | copy-start | bytes 294916
  22.3 8.0 %collective-permute-start.2 = (bf16[2,4,128,128]{3,2,1,0:T(8,128)(2,1)S(1)}, bf16[2,4,128,128]{3,2,1,0:T(8,128)(2,1)S(1)}, u32[]{:S(2)}, u32[]{:S(2)}) collective-permute-start(bf16[2,4,128,128]{3,2,1,0:T(8,128)(2,1)S(1)} %slice.252), channel_id=1, source_target_pairs={{0,32},{32,64},{64,96},{96,128},{128,160},{160,192},{192,224},{224... | collective-permute-start | bytes 786440 | tf_op jit(solution)/shard_map/ppermute | solution.py:24
  30.4 0.7 copy-start.8
  31.6 6.3 %collective-permute-start.3 = (bf16[4,1,128,128]{3,2,1,0:T(8,128)(2,1)S(1)}, bf16[4,1,128,128]{3,2,1,0:T(8,128)(2,1)S(1)}, u32[]{:S(2)}, u32[]{:S(2)}) collective-permute-start(bf16[4,1,128,128]{3,2,1,0:T(8,128)(2,1)S(1)} %slice.255), channel_id=1, source_target_pairs={{0,1},{1,2},{2,3},{3,4},{4,5},{5,6},{6,7},{7,8},{8,9},{9,10},{10,1... | collective-permute-start | bytes 393224 | tf_op jit(solution)/shard_map/ppermute | solution.py:24
  41.8 1.1 copy-start.6
  42.8 6.1 %copy-start.2 = (bf16[3,256,256]{2,1,0:T(8,128)(2,1)S(1)}, bf16[3,256,256]{2,1,0:T(8,128)(2,1)}, u32[]{:S(2)}) copy-start(bf16[3,256,256]{2,1,0:T(8,128)(2,1)} %param.19) | copy-start | bytes 1179652
  43.4 6.0 %copy-start.7 = (f32[256]{0:T(256)S(1)}, f32[256]{0:T(256)}, u32[]{:S(2)}) copy-start(f32[256]{0:T(256)} %param.20) | copy-start | bytes 3076
  43.4 5.4 %collective-permute-start.4 = (bf16[1,2,64,256]{3,2,1,0:T(8,128)(2,1)S(1)}, bf16[1,2,64,256]{3,2,1,0:T(8,128)(2,1)S(1)}, u32[]{:S(2)}, u32[]{:S(2)}) collective-permute-start(bf16[1,2,64,256]{3,2,1,0:T(8,128)(2,1)S(1)} %slice.256), channel_id=1, source_target_pairs={{0,32},{32,64},{64,96},{96,128},{128,160},{160,192},{192,224},{224... | collective-permute-start | bytes 196616 | tf_op jit(solution)/shard_map/ppermute | solution.py:24
  49.1 8.0 %copy-start.9 = (s32[16]{0:T(128)S(1)}, s32[16]{0:T(128)}, u32[]{:S(2)}) copy-start(s32[16]{0:T(128)} %param.14) | copy-start | bytes 196
  49.6 6.5 %collective-permute-start.5 = (bf16[2,2,64,256]{3,2,1,0:T(8,128)(2,1)S(1)}, bf16[2,2,64,256]{3,2,1,0:T(8,128)(2,1)S(1)}, u32[]{:S(2)}, u32[]{:S(2)}) collective-permute-start(bf16[2,2,64,256]{3,2,1,0:T(8,128)(2,1)S(1)} %bitcast.94), channel_id=1, source_target_pairs={{0,32},{32,64},{64,96},{96,128},{128,160},{160,192},{192,224},{224... | collective-permute-start | bytes 393224 | tf_op jit(solution)/shard_map/ppermute | solution.py:24
  142.3 7.2 %collective-permute-start.6 = (bf16[4,1,64,256]{3,2,1,0:T(8,128)(2,1)S(1)}, bf16[4,1,64,256]{3,2,1,0:T(8,128)(2,1)S(1)}, u32[]{:S(2)}, u32[]{:S(2)}) collective-permute-start(bf16[4,1,64,256]{3,2,1,0:T(8,128)(2,1)S(1)} %get-tuple-element.24), channel_id=1, source_target_pairs={{0,1},{1,2},{2,3},{3,4},{4,5},{5,6},{6,7},{7,8},{8,9},{9,10},{10,1... | collective-permute-start | bytes 393224 | tf_op jit(solution)/shard_map/ppermute | solution.py:13
  147.3 7.5 %collective-permute-start.7 = (bf16[4,1,64,256]{3,2,1,0:T(8,128)(2,1)S(1)}, bf16[4,1,64,256]{3,2,1,0:T(8,128)(2,1)S(1)}, u32[]{:S(2)}, u32[]{:S(2)}) collective-permute-start(bf16[4,1,64,256]{3,2,1,0:T(8,128)(2,1)S(1)} %get-tuple-element.25), channel_id=1, source_target_pairs={{1,0},{2,1},{3,2},{4,3},{5,4},{6,5},{7,6},{8,7},{9,8},{10,9},{11,1... | collective-permute-start | bytes 393224 | tf_op jit(solution)/shard_map/ppermute | solution.py:16
  155.4 1.0 copy-start.1
  156.2 0.7 copy-start.5
Sparse Core Ops, SparseCore 0:
  57.2 75.2 all-gather.2
where the time goes:
time: 165 us
  waiting for transfers between devices  90.9 us (55%)
  starting transfers between devices  29.6 us (18%)
  local copies, waits for them, and re-layouts  17.6 us (11%)
  between operations  14.7 us (9%)
  matrix products  7.75 us (5%)
  other arithmetic  4.09 us (2%)
    all_gather x1, waiting for transfers between devices, per_device(): lax.all_gather(flattened, 'tm', axis=0, tiled=True)  75.2 us
    ppermute x4, starting transfers between devices, passed_along(): return lax.ppermute(block, axis, route)  15.5 us
    ppermute x2, starting transfers between devices, padded_2(): lax.ppermute(lax.slice_in_dim(block, block.shape[dim] - width, None, axis...  10.3 us
    unnamed x43, local copies, waits for them, and re-layouts  10 us
    ppermute x4, waiting for transfers between devices, passed_along(): return lax.ppermute(block, axis, route)  9.56 us
    ppermute x2, waiting for transfers between devices, padded_2(): lax.ppermute(lax.slice_in_dim(block, 0, width, axis=dim), axis, backward)  6.08 us
    ppermute x2, starting transfers between devices, padded_2(): lax.ppermute(lax.slice_in_dim(block, 0, width, axis=dim), axis, backward)  3.84 us
    slice x9, local copies, waits for them, and re-layouts, spatial_conv(): padded[:, row_tap:row_tap + stride * out_rows:stride, col_tap:col_tap + s...  3.64 us
  transfers between devices with their start and end apart: 9, of which 7 were waited for; matrix products, arithmetic and copies ran while one was open for 3% of the time, Pallas kernels for 0%

commit v1 on v0

--- a/solution.py
+++ b/solution.py
@@ -150,7 +150,9 @@
     gather_fn = partial(pick_rows, owners=block_owner, my_index=my_index, block_span=block_span)
     moved_block = gather_fn(
         jnp.zeros(flattened.shape, jnp.float32),
-        lax.all_gather(flattened, "tm", axis=0, tiled=True),
+        jnp.concatenate(
+            lax.all_to_all(jnp.stack([flattened] * lax.axis_size("tm")), "tm", 0, 0), axis=0
+        ),
         jnp.int32(0),
     )
     moved_block = moved_block.astype(jnp.bfloat16).reshape(extended.shape)

time: 165 us -> 151 us (0.915)
  the two profiles are of different devices: /device:TPU:97 before, /device:TPU:93 now
where the time goes in v1:
time: 151 us; the launch traced here: 150 us
  waiting for transfers between devices  62.7 us (42%)
  starting transfers between devices  53.7 us (36%)
  local copies, waits for them, and re-layouts  20.5 us (14%)
  matrix products  7.73 us (5%)
  other arithmetic  4.09 us (3%)
    all_to_all x1, waiting for transfers between devices, per_device(): lax.all_to_all(jnp.stack([flattened] * lax.axis_size('tm')), 'tm', 0, 0)  47.5 us
    ppermute x2, starting transfers between devices, padded_2(): lax.ppermute(lax.slice_in_dim(block, block.shape[dim] - width, None, axis...  25.8 us
    ppermute x4, starting transfers between devices, passed_along(): return lax.ppermute(block, axis, route)  16.6 us
    ppermute x4, waiting for transfers between devices, passed_along(): return lax.ppermute(block, axis, route)  11.1 us
    all_to_all x1, starting transfers between devices, per_device(): lax.all_to_all(jnp.stack([flattened] * lax.axis_size('tm')), 'tm', 0, 0)  7.46 us
    reshape x1, local copies, waits for them, and re-layouts, per_device(): jnp.concatenate(lax.all_to_all(jnp.stack([flattened] * lax.axis_size('tm'...  6.98 us
    ppermute x2, waiting for transfers between devices, padded_2(): lax.ppermute(lax.slice_in_dim(block, 0, width, axis=dim), axis, backward)  4.05 us
    ppermute x2, starting transfers between devices, padded_2(): lax.ppermute(lax.slice_in_dim(block, 0, width, axis=dim), axis, backward)  3.84 us
  transfers between devices with their start and end apart: 9, of which 6 were waited for; matrix products, arithmetic and copies ran while one was open for 3% of the time, Pallas kernels for 0%

profile of v1, /device:TPU:93, one launch (start us, length us, event | category | flops | bytes accessed | tf_op | source)
XLA Modules:
  0.0 150.0 jit_solution(3786855627471090038)
XLA Ops:
  0.0 1.5 %reshape.218 = bf16[4,4,128,48]{3,2,1,0:T(8,128)(2,1)S(1)} reshape(bf16[4,4,6144]{2,1,0:T(4,128)(2,1)} %param.12) | data formatting | bytes 393216 | tf_op jit(solution)/shard_map/reshape | solution.py:117
  1.8 4.1 %collective-permute-start = (bf16[4,1,128,48]{2,3,1,0:T(8,128)(2,1)S(1)}, bf16[4,1,128,48]{2,3,1,0:T(8,128)(2,1)S(1)}, u32[]{:S(2)}, u32[]{:S(2)}) collective-permute-start(bf16[4,1,128,48]{2,3,1,0:T(8,128)(2,1)S(1)} %get-tuple-element.28), channel_id=1, source_target_pairs={{0,1},{1,2},{2,3},{3,4},{4,5},{5,6},{6,7},{7,8},{8,9},{9,10},{10,1... | collective-permute-start | bytes 147464 | tf_op jit(solution)/shard_map/ppermute | solution.py:13
  5.9 1.9 %collective-permute-start.1 = (bf16[4,1,128,48]{2,3,1,0:T(8,128)(2,1)S(1)}, bf16[4,1,128,48]{2,3,1,0:T(8,128)(2,1)S(1)}, u32[]{:S(2)}, u32[]{:S(2)}) collective-permute-start(bf16[4,1,128,48]{2,3,1,0:T(8,128)(2,1)S(1)} %get-tuple-element.29), channel_id=1, source_target_pairs={{1,0},{2,1},{3,2},{4,3},{5,4},{6,5},{7,6},{8,7},{9,8},{10,9},{11,1... | collective-permute-start | bytes 147464 | tf_op jit(solution)/shard_map/ppermute | solution.py:16
  9.3 1.3 fusion.55
  12.9 0.8 convolution_convert_fusion.1
  13.7 2.5 %collective-permute-start.2 = (bf16[2,4,128,128]{3,2,1,0:T(8,128)(2,1)S(1)}, bf16[2,4,128,128]{3,2,1,0:T(8,128)(2,1)S(1)}, u32[]{:S(2)}, u32[]{:S(2)}) collective-permute-start(bf16[2,4,128,128]{3,2,1,0:T(8,128)(2,1)S(1)} %slice.252), channel_id=1, source_target_pairs={{0,32},{32,64},{64,96},{96,128},{128,160},{160,192},{192,224},{224... | collective-permute-start | bytes 786440 | tf_op jit(solution)/shard_map/ppermute | solution.py:24
  17.0 6.4 %collective-permute-done.2 = bf16[2,4,128,128]{3,2,1,0:T(8,128)(2,1)S(1)} collective-permute-done((bf16[2,4,128,128]{3,2,1,0:T(8,128)(2,1)S(1)}, bf16[2,4,128,128]{3,2,1,0:T(8,128)(2,1)S(1)}, u32[]{:S(2)}, u32[]{:S(2)}) %collective-permute-start.2) | collective-permute-done | bytes 262176 | tf_op jit(solution)/shard_map/ppermute | solution.py:24
  24.6 3.7 %collective-permute-start.3 = (bf16[4,1,128,128]{3,2,1,0:T(8,128)(2,1)S(1)}, bf16[4,1,128,128]{3,2,1,0:T(8,128)(2,1)S(1)}, u32[]{:S(2)}, u32[]{:S(2)}) collective-permute-start(bf16[4,1,128,128]{3,2,1,0:T(8,128)(2,1)S(1)} %slice.255), channel_id=1, source_target_pairs={{0,1},{1,2},{2,3},{3,4},{4,5},{5,6},{6,7},{7,8},{8,9},{9,10},{10,1... | collective-permute-start | bytes 393224 | tf_op jit(solution)/shard_map/ppermute | solution.py:24
  28.7 1.6 %collective-permute-done.3 = bf16[4,1,128,128]{3,2,1,0:T(8,128)(2,1)S(1)} collective-permute-done((bf16[4,1,128,128]{3,2,1,0:T(8,128)(2,1)S(1)}, bf16[4,1,128,128]{3,2,1,0:T(8,128)(2,1)S(1)}, u32[]{:S(2)}, u32[]{:S(2)}) %collective-permute-start.3) | collective-permute-done | bytes 131104 | tf_op jit(solution)/shard_map/ppermute | solution.py:24
  33.4 0.8 slice.214
  35.8 4.6 %collective-permute-start.4 = (bf16[1,2,64,256]{3,2,1,0:T(8,128)(2,1)S(1)}, bf16[1,2,64,256]{3,2,1,0:T(8,128)(2,1)S(1)}, u32[]{:S(2)}, u32[]{:S(2)}) collective-permute-start(bf16[1,2,64,256]{3,2,1,0:T(8,128)(2,1)S(1)} %slice.256), channel_id=1, source_target_pairs={{0,32},{32,64},{64,96},{96,128},{128,160},{160,192},{192,224},{224... | collective-permute-start | bytes 196616 | tf_op jit(solution)/shard_map/ppermute | solution.py:24
  40.5 1.2 collective-permute-done.4
  42.5 5.8 %collective-permute-start.5 = (bf16[2,2,64,256]{3,2,1,0:T(8,128)(2,1)S(1)}, bf16[2,2,64,256]{3,2,1,0:T(8,128)(2,1)S(1)}, u32[]{:S(2)}, u32[]{:S(2)}) collective-permute-start(bf16[2,2,64,256]{3,2,1,0:T(8,128)(2,1)S(1)} %bitcast.97), channel_id=1, source_target_pairs={{0,32},{32,64},{64,96},{96,128},{128,160},{160,192},{192,224},{224... | collective-permute-start | bytes 393224 | tf_op jit(solution)/shard_map/ppermute | solution.py:24
  48.3 1.9 %collective-permute-done.5 = bf16[2,2,64,256]{3,2,1,0:T(8,128)(2,1)S(1)} collective-permute-done((bf16[2,2,64,256]{3,2,1,0:T(8,128)(2,1)S(1)}, bf16[2,2,64,256]{3,2,1,0:T(8,128)(2,1)S(1)}, u32[]{:S(2)}, u32[]{:S(2)}) %collective-permute-start.5) | collective-permute-done | bytes 131104 | tf_op jit(solution)/shard_map/ppermute | solution.py:24
  50.5 3.6 %stack.3 = bf16[16,4,32768]{2,1,0:T(4,128)(2,1)} broadcast(bf16[4,32768]{1,0:T(4,128)(2,1)S(1)} %bitcast.86), dimensions={1,2} | broadcast | bytes 4456448 | tf_op jit(solution)/shard_map/stack | solution.py:154
  54.0 7.5 %all-to-all-start = ((bf16[16,4,32768]{2,1,0:T(4,128)(2,1)}), bf16[16,4,32768]{2,1,0:T(4,128)(2,1)}, u32[]{:S(2)}, u32[]{:S(2)}) async-start(bf16[16,4,32768]{2,1,0:T(4,128)(2,1)} %stack.3), calls=%async_computation | async-start | bytes 8388608 | tf_op jit(solution)/shard_map/all_to_all | solution.py:154
  61.7 47.5 %all-to-all-done = bf16[16,4,32768]{2,1,0:T(4,128)(2,1)} async-done(((bf16[16,4,32768]{2,1,0:T(4,128)(2,1)}), bf16[16,4,32768]{2,1,0:T(4,128)(2,1)}, u32[]{:S(2)}, u32[]{:S(2)}) %all-to-all-start) | async-done | bytes 4194336 | tf_op jit(solution)/shard_map/all_to_all | solution.py:154
  109.2 7.0 %reshape.231 = bf16[64,32768]{1,0:T(8,128)(2,1)} reshape(bf16[16,4,32768]{2,1,0:T(4,128)(2,1)} %all-to-all-done) | data formatting | bytes 8388608 | tf_op jit(solution)/shard_map/reshape | solution.py:153
  116.2 2.8 %convolution_convert_fusion = bf16[4,32768]{1,0:T(4,128)(2,1)S(1)} fusion(bf16[64,32768]{1,0:T(8,128)(2,1)} %reshape.231, s32[64]{0:T(128)S(1)} %and_select_fusion.3, pred[64]{0:T(512)(128)(4,1)S(1)} %broadcast_compare_fusion), kind=kOutput, calls=%fused_computation | convolution fusion | flops 16908800 | bytes 4456768 | tf_op jit(solution)/shard_map/dot_general | solution.py:90
  119.1 21.6 %collective-permute-start.6 = (bf16[4,1,64,256]{3,2,1,0:T(8,128)(2,1)S(1)}, bf16[4,1,64,256]{3,2,1,0:T(8,128)(2,1)S(1)}, u32[]{:S(2)}, u32[]{:S(2)}) collective-permute-start(bf16[4,1,64,256]{3,2,1,0:T(8,128)(2,1)S(1)} %get-tuple-element.24), channel_id=1, source_target_pairs={{0,1},{1,2},{2,3},{3,4},{4,5},{5,6},{6,7},{7,8},{8,9},{9,10},{10,1... | collective-permute-start | bytes 393224 | tf_op jit(solution)/shard_map/ppermute | solution.py:13
  140.7 1.9 %collective-permute-start.7 = (bf16[4,1,64,256]{3,2,1,0:T(8,128)(2,1)S(1)}, bf16[4,1,64,256]{3,2,1,0:T(8,128)(2,1)S(1)}, u32[]{:S(2)}, u32[]{:S(2)}) collective-permute-start(bf16[4,1,64,256]{3,2,1,0:T(8,128)(2,1)S(1)} %get-tuple-element.25), channel_id=1, source_target_pairs={{1,0},{2,1},{3,2},{4,3},{5,4},{6,5},{7,6},{8,7},{9,8},{10,9},{11,1... | collective-permute-start | bytes 393224 | tf_op jit(solution)/shard_map/ppermute | solution.py:16
  143.0 4.1 %collective-permute-done.7 = bf16[4,1,64,256]{3,2,1,0:T(8,128)(2,1)S(1)} collective-permute-done((bf16[4,1,64,256]{3,2,1,0:T(8,128)(2,1)S(1)}, bf16[4,1,64,256]{3,2,1,0:T(8,128)(2,1)S(1)}, u32[]{:S(2)}, u32[]{:S(2)}) %collective-permute-start.7) | collective-permute-done | bytes 131104 | tf_op jit(solution)/shard_map/ppermute | solution.py:16
  147.6 0.8 convolution_convert_fusion.2
  149.1 0.8 fusion.7
  (113 shorter events, 12.8 us)
Async XLA Ops:
  0.0 147.6 %copy-start = (bf16[3,3,256,256]{3,2,1,0:T(8,128)(2,1)S(1)}, bf16[3,3,256,256]{3,2,1,0:T(8,128)(2,1)}, u32[]{:S(2)}) copy-start(bf16[3,3,256,256]{3,2,1,0:T(8,128)(2,1)} %param.21) | copy-start | bytes 3538948
  1.8 9.9 %collective-permute-start = (bf16[4,1,128,48]{2,3,1,0:T(8,128)(2,1)S(1)}, bf16[4,1,128,48]{2,3,1,0:T(8,128)(2,1)S(1)}, u32[]{:S(2)}, u32[]{:S(2)}) collective-permute-start(bf16[4,1,128,48]{2,3,1,0:T(8,128)(2,1)S(1)} %get-tuple-element.28), channel_id=1, source_target_pairs={{0,1},{1,2},{2,3},{3,4},{4,5},{5,6},{6,7},{7,8},{8,9},{9,10},{10,1... | collective-permute-start | bytes 147464 | tf_op jit(solution)/shard_map/ppermute | solution.py:13
  5.9 5.8 %collective-permute-start.1 = (bf16[4,1,128,48]{2,3,1,0:T(8,128)(2,1)S(1)}, bf16[4,1,128,48]{2,3,1,0:T(8,128)(2,1)S(1)}, u32[]{:S(2)}, u32[]{:S(2)}) collective-permute-start(bf16[4,1,128,48]{2,3,1,0:T(8,128)(2,1)S(1)} %get-tuple-element.29), channel_id=1, source_target_pairs={{1,0},{2,1},{3,2},{4,3},{5,4},{6,5},{7,6},{8,7},{9,8},{10,9},{11,1... | collective-permute-start | bytes 147464 | tf_op jit(solution)/shard_map/ppermute | solution.py:16
  12.0 0.9 copy-start.3
  13.7 9.8 %copy-start.4 = (bf16[3,128,128]{2,1,0:T(8,128)(2,1)S(1)}, bf16[3,128,128]{2,1,0:T(8,128)(2,1)}, u32[]{:S(2)}) copy-start(bf16[3,128,128]{2,1,0:T(8,128)(2,1)} %param.16) | copy-start | bytes 294916
  13.7 9.6 %collective-permute-start.2 = (bf16[2,4,128,128]{3,2,1,0:T(8,128)(2,1)S(1)}, bf16[2,4,128,128]{3,2,1,0:T(8,128)(2,1)S(1)}, u32[]{:S(2)}, u32[]{:S(2)}) collective-permute-start(bf16[2,4,128,128]{3,2,1,0:T(8,128)(2,1)S(1)} %slice.252), channel_id=1, source_target_pairs={{0,32},{32,64},{64,96},{96,128},{128,160},{160,192},{192,224},{224... | collective-permute-start | bytes 786440 | tf_op jit(solution)/shard_map/ppermute | solution.py:24
  23.5 0.7 copy-start.8
  24.6 5.7 %collective-permute-start.3 = (bf16[4,1,128,128]{3,2,1,0:T(8,128)(2,1)S(1)}, bf16[4,1,128,128]{3,2,1,0:T(8,128)(2,1)S(1)}, u32[]{:S(2)}, u32[]{:S(2)}) collective-permute-start(bf16[4,1,128,128]{3,2,1,0:T(8,128)(2,1)S(1)} %slice.255), channel_id=1, source_target_pairs={{0,1},{1,2},{2,3},{3,4},{4,5},{5,6},{6,7},{7,8},{8,9},{9,10},{10,1... | collective-permute-start | bytes 393224 | tf_op jit(solution)/shard_map/ppermute | solution.py:24
  34.2 1.1 copy-start.6
  35.3 6.6 %copy-start.2 = (bf16[3,256,256]{2,1,0:T(8,128)(2,1)S(1)}, bf16[3,256,256]{2,1,0:T(8,128)(2,1)}, u32[]{:S(2)}) copy-start(bf16[3,256,256]{2,1,0:T(8,128)(2,1)} %param.19) | copy-start | bytes 1179652
  35.8 6.4 %copy-start.7 = (f32[256]{0:T(256)S(1)}, f32[256]{0:T(256)}, u32[]{:S(2)}) copy-start(f32[256]{0:T(256)} %param.20) | copy-start | bytes 3076
  35.8 5.9 %collective-permute-start.4 = (bf16[1,2,64,256]{3,2,1,0:T(8,128)(2,1)S(1)}, bf16[1,2,64,256]{3,2,1,0:T(8,128)(2,1)S(1)}, u32[]{:S(2)}, u32[]{:S(2)}) collective-permute-start(bf16[1,2,64,256]{3,2,1,0:T(8,128)(2,1)S(1)} %slice.256), channel_id=1, source_target_pairs={{0,32},{32,64},{64,96},{96,128},{128,160},{160,192},{192,224},{224... | collective-permute-start | bytes 196616 | tf_op jit(solution)/shard_map/ppermute | solution.py:24
  42.5 7.7 %collective-permute-start.5 = (bf16[2,2,64,256]{3,2,1,0:T(8,128)(2,1)S(1)}, bf16[2,2,64,256]{3,2,1,0:T(8,128)(2,1)S(1)}, u32[]{:S(2)}, u32[]{:S(2)}) collective-permute-start(bf16[2,2,64,256]{3,2,1,0:T(8,128)(2,1)S(1)} %bitcast.97), channel_id=1, source_target_pairs={{0,32},{32,64},{64,96},{96,128},{128,160},{160,192},{192,224},{224... | collective-permute-start | bytes 393224 | tf_op jit(solution)/shard_map/ppermute | solution.py:24
  54.0 7.6 %copy-start.9 = (s32[16]{0:T(128)S(1)}, s32[16]{0:T(128)}, u32[]{:S(2)}) copy-start(s32[16]{0:T(128)} %param.14) | copy-start | bytes 196
  54.0 55.2 %all-to-all-start = ((bf16[16,4,32768]{2,1,0:T(4,128)(2,1)}), bf16[16,4,32768]{2,1,0:T(4,128)(2,1)}, u32[]{:S(2)}, u32[]{:S(2)}) async-start(bf16[16,4,32768]{2,1,0:T(4,128)(2,1)} %stack.3), calls=%async_computation | async-start | bytes 8388608 | tf_op jit(solution)/shard_map/all_to_all | solution.py:154
  119.1 23.9 %collective-permute-start.6 = (bf16[4,1,64,256]{3,2,1,0:T(8,128)(2,1)S(1)}, bf16[4,1,64,256]{3,2,1,0:T(8,128)(2,1)S(1)}, u32[]{:S(2)}, u32[]{:S(2)}) collective-permute-start(bf16[4,1,64,256]{3,2,1,0:T(8,128)(2,1)S(1)} %get-tuple-element.24), channel_id=1, source_target_pairs={{0,1},{1,2},{2,3},{3,4},{4,5},{5,6},{6,7},{7,8},{8,9},{9,10},{10,1... | collective-permute-start | bytes 393224 | tf_op jit(solution)/shard_map/ppermute | solution.py:13
  140.7 6.3 %collective-permute-start.7 = (bf16[4,1,64,256]{3,2,1,0:T(8,128)(2,1)S(1)}, bf16[4,1,64,256]{3,2,1,0:T(8,128)(2,1)S(1)}, u32[]{:S(2)}, u32[]{:S(2)}) collective-permute-start(bf16[4,1,64,256]{3,2,1,0:T(8,128)(2,1)S(1)} %get-tuple-element.25), channel_id=1, source_target_pairs={{1,0},{2,1},{3,2},{4,3},{5,4},{6,5},{7,6},{8,7},{9,8},{10,9},{11,1... | collective-permute-start | bytes 393224 | tf_op jit(solution)/shard_map/ppermute | solution.py:16
  147.6 1.0 copy-start.1
  148.4 0.7 copy-start.5
